TPU v7x, 32 devices: a whole 2x2x4 slice. The times are simulated.
32 devices in a mesh: frame: 4 (over z), patch: 8 (over y, x, core).
Axes of the slice: x: 2, y: 2, z: 4, core: 2. Of those that a mesh axis runs over, the one named last changes fastest.
Arguments:
- latent: bfloat16 [8192, 1536], P(('frame', 'patch')), parts along dimension 0, may hold values from -6 to 6
- conv_weight: float32 [9, 1536], replicated, may hold values from -4 to 4
- time_table: bfloat16 [50, 4608], replicated
- action_table: bfloat16 [18, 4608], replicated
- timestep: int32 [4], P('frame'), parts along dimension 0, may hold values from 0 to 49
- action: int32 [4], P('frame'), parts along dimension 0, may hold values from 0 to 17
- w_qkv: bfloat16 [1536, 4608], replicated, may hold values from -0.21875 to 0.21875
- w_out: bfloat16 [1536, 1536], replicated, may hold values from -0.15625 to 0.15625
- stale_kv: bfloat16 [8192, 3072], P(('frame', 'patch')), parts along dimension 0
Outputs:
- layer_out: bfloat16 [8192, 1536], P(('frame', 'patch')), parts along dimension 0
- fresh_kv: bfloat16 [8192, 3072], P(('frame', 'patch')), parts along dimension 0
There are 4 independent parts, one for each index of `frame`. A program takes and returns all parts, laid end to end along the dimension named above; an argument that names none is the same for every part. Nothing has to cross between parts.
All inputs are finite; a program needn't handle non-finite values.
Results may differ from a plain program's by a relative error of at most 0.012.
Values may be sent and summed in bfloat16 or wider, within the bound.
A program may use at most 128 MiB of HBM per device.

v0:
```python
import jax
import jax.numpy as jnp
from jax import lax
from jax.sharding import PartitionSpec as P

HEADS = 24
GRID_W = 64


def padded_2(block, sides, width):
    for axis, dim in sides:
        count = lax.axis_size(axis)
        forward = [(i, i + 1) for i in range(count - 1)]
        backward = [(target, source) for source, target in forward]
        low = lax.ppermute(
            lax.slice_in_dim(block, block.shape[dim] - width, None, axis=dim), axis, forward
        )
        high = lax.ppermute(lax.slice_in_dim(block, 0, width, axis=dim), axis, backward)
        block = jnp.concatenate([low, block, high], axis=dim)
    return block


def lookup(table, index):
    hot = (jnp.arange(table.shape[0], dtype=jnp.int32)[None, :] == index[:, None]).astype(
        table.dtype
    )
    return jnp.dot(hot, table, preferred_element_type=jnp.float32)[0]


def attend(carry, piece, start, query, own_start, own_rows):
    width = piece.shape[1] // 2
    heads = query.shape[1]
    size = query.shape[2]
    count_rows = piece.shape[0]
    block = 512

    def step(turn, state):
        top, total, acc = state
        part_kv = lax.dynamic_slice_in_dim(piece, turn * block, block, 0)
        keys = part_kv[:, :width].reshape(block, heads, size)
        values = part_kv[:, width:].reshape(block, heads, size)
        scores = jnp.einsum(
            "qhe,khe->hqk", query, keys, preferred_element_type=jnp.float32
        ) * size ** (-0.5)
        index_rows = start + turn * block + jnp.arange(block, dtype=jnp.int32)
        inside = (index_rows >= own_start) & (index_rows < own_start + own_rows)
        scores = jnp.where(inside[None, None, :], -jnp.inf, scores)
        new_top = jnp.maximum(top, jnp.max(scores, axis=2))
        factor = jnp.exp(top - new_top)
        expo = jnp.exp(scores - new_top[:, :, None])
        total = total * factor + jnp.sum(expo, axis=2)
        acc = acc * factor[:, :, None] + jnp.einsum(
            "hqk,khe->hqe", expo.astype(jnp.bfloat16), values, preferred_element_type=jnp.float32
        )
        return (new_top, total, acc)

    return lax.fori_loop(0, count_rows // block, step, carry)


def per_device(
    latent, conv_weight, time_table, action_table, timestep, action, w_qkv, w_out, stale_kv
):
    rows, width = latent.shape
    grid = latent.reshape(rows // GRID_W, GRID_W, width)
    extended = padded_2(grid, (("patch", 0),), 1)
    padded = jnp.pad(extended, ((0, 0), (1, 1), (0, 0)))
    nrows = grid.shape[0]
    mixed = grid.astype(jnp.float32)
    for a in range(3):
        for b in range(3):
            mixed = (
                mixed
                + padded[a : a + nrows, b : b + GRID_W].astype(jnp.float32) * conv_weight[3 * a + b]
            )
    mixed = mixed.reshape(rows, width)
    modulation = lookup(time_table, timestep) + lookup(action_table, action)
    shift = modulation[:width]
    scale = modulation[width : 2 * width]
    gate = modulation[2 * width :]
    mean = jnp.mean(mixed, axis=1, keepdims=True)
    var = jnp.mean((mixed - mean) ** 2, axis=1, keepdims=True)
    normed = ((mixed - mean) * lax.rsqrt(var + 1e-06) * (1.0 + scale) + shift).astype(jnp.bfloat16)
    projected = jnp.dot(normed, w_qkv, preferred_element_type=jnp.float32)
    fresh_kv = projected[:, width:].astype(jnp.bfloat16)
    heads = HEADS
    size = width // heads
    query = projected[:, :width].astype(jnp.bfloat16).reshape(rows, heads, size)
    own_keys = fresh_kv[:, :width].reshape(rows, heads, size)
    own_values = fresh_kv[:, width:].reshape(rows, heads, size)
    own_scores = jnp.einsum(
        "qhe,khe->hqk", query, own_keys, preferred_element_type=jnp.float32
    ) * size ** (-0.5)
    top = jnp.max(own_scores, axis=2)
    expo = jnp.exp(own_scores - top[:, :, None])
    total = jnp.sum(expo, axis=2)
    acc = jnp.einsum(
        "hqk,khe->hqe", expo.astype(jnp.bfloat16), own_values, preferred_element_type=jnp.float32
    )
    own_start = lax.axis_index("patch") * rows
    whole = lax.all_gather(stale_kv, "patch", axis=0, tiled=True)
    top, total, acc = attend((top, total, acc), whole, 0, query, own_start, rows)
    result = acc / total[:, :, None]
    attended = jnp.transpose(result, (1, 0, 2)).reshape(rows, width).astype(jnp.bfloat16)
    proj = jnp.dot(attended, w_out, preferred_element_type=jnp.float32)
    layer_out = (mixed + gate * proj).astype(jnp.bfloat16)
    return (layer_out, fresh_kv)


def solution(mesh):
    in_specs = (
        P(("frame", "patch"), None),
        P(),
        P(),
        P(),
        P("frame"),
        P("frame"),
        P(),
        P(),
        P(("frame", "patch"), None),
    )
    out_specs = (P(("frame", "patch"), None), P(("frame", "patch"), None))
    return jax.shard_map(
        per_device, mesh=mesh, in_specs=in_specs, out_specs=out_specs, check_vma=False
    )
```

profile of v0, /device:TPU:0, one launch (start us, length us, event | category | flops | bytes accessed | tf_op | source)
XLA Modules:
  0.0 153.8 jit_solution(15883436996087473038)
XLA Ops:
  7.2 2.7 %copy.23 = bf16[256,3072]{0,1:T(8,128)(2,1)} copy(bf16[256,3072]{1,0:T(8,128)(2,1)} %param.19) | data formatting | bytes 3145728 | tf_op args[8]
  11.0 2.4 %collective-permute-start = (bf16[1,64,1536]{2,1,0:T(8,128)(2,1)S(1)}, bf16[1,64,1536]{2,1,0:T(8,128)(2,1)S(1)}, u32[]{:S(2)}, u32[]{:S(2)}) collective-permute-start(bf16[1,64,1536]{2,1,0:T(8,128)(2,1)S(1)} %get-tuple-element.206), channel_id=1, source_target_pairs={{0,1},{1,2},{2,3},{3,4},{4,5},{5,6},{6,7},{8,9},{9,10},{10,11},{11... | collective-permute-start | bytes 589832 | tf_op jit(solution)/shard_map/ppermute | solution.py:15
  16.6 2.2 %collective-permute-done.1 = bf16[1,64,1536]{2,1,0:T(8,128)(2,1)S(1)} collective-permute-done((bf16[1,64,1536]{2,1,0:T(8,128)(2,1)S(1)}, bf16[1,64,1536]{2,1,0:T(8,128)(2,1)S(1)}, u32[]{:S(2)}, u32[]{:S(2)}) %collective-permute-start.1) | collective-permute-done | bytes 196640 | tf_op jit(solution)/shard_map/ppermute | solution.py:18
  19.2 2.4 %fusion.48 = (f32[4,64]{1,0:T(4,128)S(1)}, f32[4,64,1536]{2,1,0:T(8,128)S(1)}) fusion(f32[1536]{0:T(1024)S(1)} %get-tuple-element.177, bf16[6,66,1536]{2,1,0:T(8,128)(2,1)S(1)} %fusion.38, f32[1536]{0:T(1024)S(1)} %get-tuple-element.178, bf16[1,64,1536]{2,1,0:T(8,128)(2,1)S(1)} %collective-permute-done.1, bf16[4,64,1536]{2,1,0:T(8,128)(2,1)S(1)} %bitcast.79, ...), kind=kLoop, calls=%fused_computation.81 | loop fusion | flops 11796224 | bytes 7527424 | tf_op jit(solution)/shard_map/reduce_sum | solution.py:80
  22.5 9.6 %convolution_convert_fusion = bf16[256,4608]{1,0:T(8,128)(2,1)S(1)} fusion(bf16[256,1536]{1,0:T(8,128)(2,1)S(1)} %fusion.33, bf16[1536,4608]{1,0:T(8,128)(2,1)} %param.17), kind=kOutput, calls=%fused_computation.18 | convolution fusion | flops 3625058304 | bytes 17301504 | tf_op jit(solution)/shard_map/dot_general | solution.py:83
  34.8 2.3 %copy.21 = bf16[256,1536]{0,1:T(8,128)(2,1)} copy(bf16[256,1536]{1,0:T(8,128)(2,1)} %get-tuple-element.203) | data formatting | bytes 1572864 | tf_op jit(solution)/shard_map/slice | solution.py:89
  39.6 2.2 %multiply_reduce_fusion = (f32[24,256]{1,0:T(8,128)S(1)}, f32[24,256,256]{1,2,0:T(8,128)S(1)}) fusion(bf16[256,24,64]{0,2,1:T(8,128)(2,1)S(1)} %bitcast.75, bf16[256,24,64]{0,2,1:T(8,128)(2,1)} %bitcast.81), kind=kOutput, calls=%fused_computation.20 | convolution fusion | flops 204466176 | bytes 7888896 | tf_op jit(solution)/shard_map/qhe,khe->hqk/dot_general | solution.py:90
  42.9 2.3 %fusion.15 = f32[24,256,64]{1,2,0:T(8,128)} fusion(bf16[256,24,64]{0,2,1:T(8,128)(2,1)S(1)} %bitcast.80, f32[24,256,256]{1,2,0:T(8,128)S(1)} %get-tuple-element.212, f32[24,256]{1,0:T(8,128)S(1)} %get-tuple-element.275), kind=kOutput, calls=%fused_computation.25 | convolution fusion | flops 206045184 | bytes 8675328 | tf_op jit(solution)/shard_map/hqk,khe->hqe/dot_general | solution.py:96
  45.3 42.3 %all-gather.2.cloned.1.call-done = bf16[2048,3072]{0,1:T(8,128)(2,1)} async-done(((bf16[256,3072]{0,1:T(8,128)(2,1)}), bf16[2048,3072]{0,1:T(8,128)(2,1)}) %all-gather.2.cloned.1.call-update) | async-done | bytes 12582928 | tf_op jit(solution)/shard_map/all_gather | solution.py:100
  87.6 53.1 %while.18 = (s32[]{:T(128)}, f32[24,256]{1,0:T(8,128)S(1)}, f32[24,256]{1,0:T(8,128)S(1)}, f32[24,256,64]{1,2,0:T(8,128)}, s32[]{:T(128)}, /*index=5*/s32[]{:T(1...) while((s32[]{:T(128)}, f32[24,256]{1,0:T(8,128)S(1)}, ...), condition=%wide.region_7.8_spmd, body=%wide.region_4.7_spmd.sunk | while | flops 840710144 | bytes 51513544 | solution.py:57
  89.7 3.0 %bitcast_reduce_fusion.2 = (f32[24,256]{1,0:T(8,128)S(1)}, f32[24,512,256]{2,1,0:T(8,128)S(1)}) fusion(pred[512]{0:T(512)(128)(4,1)S(1)} %fusion.76, bf16[512,24,64]{0,2,1:T(8,128)(2,1)S(1)} %bitcast.73, bf16[256,24,64]{0,2,1:T(8,128)(2,1)S(1)} %get-tuple-element.307), kind=kOutput, calls=%fused_computation.1.clone.1 | convolution fusion | flops 412084224 | bytes 14967296 | tf_op jit(solution)/shard_map/while/body/eval_jaxpr/qhe,khe->hqk/dot_general | solution.py:42
  92.7 2.6 %fusion.78 = f32[24,256]{1,0:T(8,128)S(1)} fusion(f32[24,512,256]{2,1,0:T(8,128)S(1)} %get-tuple-element.270, f32[24,256]{1,0:T(8,128)S(1)} %max.9, pred[512]{0:T(512)(128)(4,1)S(1)} %fusion.76), kind=kLoop, calls=%fused_computation.5.clone.1 | loop fusion | flops 12576768 | bytes 12632576 | tf_op jit(solution)/shard_map/while/body/eval_jaxpr/reduce_sum | solution.py:51
  95.4 5.5 %multiply_add_fusion.5 = f32[24,256,64]{1,2,0:T(8,128)} fusion(f32[24,256,64]{1,2,0:T(8,128)} %get-tuple-element.290, bf16[512,24,64]{0,2,1:T(8,128)(2,1)S(1)} %bitcast.74, f32[24,512,256]{2,1,0:T(8,128)S(1)} %get-tuple-element.270, f32[24,256]{1,0:T(8,128)S(1)} %max.9, pred[512]{0:T(512)(128)(4,1)S(1)} %fusion.76, f32[24,256]{1,0:T(8,128)S(1)} %get-tuple-element.273), kind=kOutput, calls=%fused_computation.8.clone.1 | convolution fusion | flops 416022528 | bytes 17351168 | tf_op jit(solution)/shard_map/while/body/eval_jaxpr/hqk,khe->hqe/dot_general | solution.py:52
  100.9 2.1 %fusion.77 = (bf16[512,1536]{0,1:T(8,128)(2,1)S(1)}, bf16[512,1536]{0,1:T(8,128)(2,1)S(1)}) fusion(bf16[2048,3072]{0,1:T(8,128)(2,1)} %get-tuple-element.306, s32[]{:T(128)S(6)} %select_n.39, s32[]{:T(128)S(6)} %add.285), kind=kLoop, calls=%fused_computation.82.clone.1 | loop fusion | bytes 6291464 | tf_op jit(solution)/shard_map/while/body/eval_jaxpr/slice | solution.py:41
  103.0 3.0 %bitcast_reduce_fusion.2 = (f32[24,256]{1,0:T(8,128)S(1)}, f32[24,512,256]{2,1,0:T(8,128)S(1)}) fusion(pred[512]{0:T(512)(128)(4,1)S(1)} %fusion.76, bf16[512,24,64]{0,2,1:T(8,128)(2,1)S(1)} %bitcast.73, bf16[256,24,64]{0,2,1:T(8,128)(2,1)S(1)} %get-tuple-element.307), kind=kOutput, calls=%fused_computation.1.clone.1 | convolution fusion | flops 412084224 | bytes 14967296 | tf_op jit(solution)/shard_map/while/body/eval_jaxpr/qhe,khe->hqk/dot_general | solution.py:42
  106.0 2.6 %fusion.78 = f32[24,256]{1,0:T(8,128)S(1)} fusion(f32[24,512,256]{2,1,0:T(8,128)S(1)} %get-tuple-element.270, f32[24,256]{1,0:T(8,128)S(1)} %max.9, pred[512]{0:T(512)(128)(4,1)S(1)} %fusion.76), kind=kLoop, calls=%fused_computation.5.clone.1 | loop fusion | flops 12576768 | bytes 12632576 | tf_op jit(solution)/shard_map/while/body/eval_jaxpr/reduce_sum | solution.py:51
  108.6 5.5 %multiply_add_fusion.5 = f32[24,256,64]{1,2,0:T(8,128)} fusion(f32[24,256,64]{1,2,0:T(8,128)} %get-tuple-element.290, bf16[512,24,64]{0,2,1:T(8,128)(2,1)S(1)} %bitcast.74, f32[24,512,256]{2,1,0:T(8,128)S(1)} %get-tuple-element.270, f32[24,256]{1,0:T(8,128)S(1)} %max.9, pred[512]{0:T(512)(128)(4,1)S(1)} %fusion.76, f32[24,256]{1,0:T(8,128)S(1)} %get-tuple-element.273), kind=kOutput, calls=%fused_computation.8.clone.1 | convolution fusion | flops 416022528 | bytes 17351168 | tf_op jit(solution)/shard_map/while/body/eval_jaxpr/hqk,khe->hqe/dot_general | solution.py:52
  116.3 3.0 %bitcast_reduce_fusion.2 = (f32[24,256]{1,0:T(8,128)S(1)}, f32[24,512,256]{2,1,0:T(8,128)S(1)}) fusion(pred[512]{0:T(512)(128)(4,1)S(1)} %fusion.76, bf16[512,24,64]{0,2,1:T(8,128)(2,1)S(1)} %bitcast.73, bf16[256,24,64]{0,2,1:T(8,128)(2,1)S(1)} %get-tuple-element.307), kind=kOutput, calls=%fused_computation.1.clone.1 | convolution fusion | flops 412084224 | bytes 14967296 | tf_op jit(solution)/shard_map/while/body/eval_jaxpr/qhe,khe->hqk/dot_general | solution.py:42
  119.3 2.6 %fusion.78 = f32[24,256]{1,0:T(8,128)S(1)} fusion(f32[24,512,256]{2,1,0:T(8,128)S(1)} %get-tuple-element.270, f32[24,256]{1,0:T(8,128)S(1)} %max.9, pred[512]{0:T(512)(128)(4,1)S(1)} %fusion.76), kind=kLoop, calls=%fused_computation.5.clone.1 | loop fusion | flops 12576768 | bytes 12632576 | tf_op jit(solution)/shard_map/while/body/eval_jaxpr/reduce_sum | solution.py:51
  121.9 5.5 %multiply_add_fusion.5 = f32[24,256,64]{1,2,0:T(8,128)} fusion(f32[24,256,64]{1,2,0:T(8,128)} %get-tuple-element.290, bf16[512,24,64]{0,2,1:T(8,128)(2,1)S(1)} %bitcast.74, f32[24,512,256]{2,1,0:T(8,128)S(1)} %get-tuple-element.270, f32[24,256]{1,0:T(8,128)S(1)} %max.9, pred[512]{0:T(512)(128)(4,1)S(1)} %fusion.76, f32[24,256]{1,0:T(8,128)S(1)} %get-tuple-element.273), kind=kOutput, calls=%fused_computation.8.clone.1 | convolution fusion | flops 416022528 | bytes 17351168 | tf_op jit(solution)/shard_map/while/body/eval_jaxpr/hqk,khe->hqe/dot_general | solution.py:52
  129.5 3.0 %bitcast_reduce_fusion.2 = (f32[24,256]{1,0:T(8,128)S(1)}, f32[24,512,256]{2,1,0:T(8,128)S(1)}) fusion(pred[512]{0:T(512)(128)(4,1)S(1)} %fusion.76, bf16[512,24,64]{0,2,1:T(8,128)(2,1)S(1)} %bitcast.73, bf16[256,24,64]{0,2,1:T(8,128)(2,1)S(1)} %get-tuple-element.307), kind=kOutput, calls=%fused_computation.1.clone.1 | convolution fusion | flops 412084224 | bytes 14967296 | tf_op jit(solution)/shard_map/while/body/eval_jaxpr/qhe,khe->hqk/dot_general | solution.py:42
  132.6 2.6 %fusion.78 = f32[24,256]{1,0:T(8,128)S(1)} fusion(f32[24,512,256]{2,1,0:T(8,128)S(1)} %get-tuple-element.270, f32[24,256]{1,0:T(8,128)S(1)} %max.9, pred[512]{0:T(512)(128)(4,1)S(1)} %fusion.76), kind=kLoop, calls=%fused_computation.5.clone.1 | loop fusion | flops 12576768 | bytes 12632576 | tf_op jit(solution)/shard_map/while/body/eval_jaxpr/reduce_sum | solution.py:51
  135.2 5.5 %multiply_add_fusion.5 = f32[24,256,64]{1,2,0:T(8,128)} fusion(f32[24,256,64]{1,2,0:T(8,128)} %get-tuple-element.290, bf16[512,24,64]{0,2,1:T(8,128)(2,1)S(1)} %bitcast.74, f32[24,512,256]{2,1,0:T(8,128)S(1)} %get-tuple-element.270, f32[24,256]{1,0:T(8,128)S(1)} %max.9, pred[512]{0:T(512)(128)(4,1)S(1)} %fusion.76, f32[24,256]{1,0:T(8,128)S(1)} %get-tuple-element.273), kind=kOutput, calls=%fused_computation.8.clone.1 | convolution fusion | flops 416022528 | bytes 17351168 | tf_op jit(solution)/shard_map/while/body/eval_jaxpr/hqk,khe->hqe/dot_general | solution.py:52
  142.3 4.7 %fusion.21 = bf16[256,1536]{1,0:T(8,128)(2,1)} fusion(f32[256,1536]{1,0:T(8,128)S(1)} %bitcast.77, bf16[256,1536]{0,1:T(8,128)(2,1)S(1)} %bitcast.82, bf16[1536,1536]{1,0:T(8,128)(2,1)} %param.18, f32[1536]{0:T(1024)S(1)} %get-tuple-element.208), kind=kOutput, calls=%fused_computation.31 | convolution fusion | flops 1209139200 | bytes 7870464 | tf_op jit(solution)/shard_map/dot_general | solution.py:104
  (54 shorter events, 18.6 us)
Async XLA Ops:
  7.2 9.1 %copy-start = (bf16[50,4608]{1,0:T(8,128)(2,1)S(1)}, bf16[50,4608]{1,0:T(8,128)(2,1)}, u32[]{:S(2)}) copy-start(bf16[50,4608]{1,0:T(8,128)(2,1)} %param.13) | copy-start | bytes 1382404
  7.2 80.4 %all-gather.2.cloned.1.call-start = ((), (), s32[]{:S(2)}) async-start(), calls=%async_computation | async-start | bytes 14155776 | tf_op jit(solution)/shard_map/all_gather | solution.py:100
  9.9 1.1 copy-start.2
  9.9 6.1 %copy-start.4 = (bf16[18,4608]{1,0:T(8,128)(2,1)S(1)}, bf16[18,4608]{1,0:T(8,128)(2,1)}, u32[]{:S(2)}) copy-start(bf16[18,4608]{1,0:T(8,128)(2,1)} %param.14) | copy-start | bytes 497668
  9.9 6.6 %copy-start.5 = (f32[9,1536]{1,0:T(8,128)S(1)}, f32[9,1536]{1,0:T(8,128)}, u32[]{:S(2)}) copy-start(f32[9,1536]{1,0:T(8,128)} %param.12) | copy-start | bytes 165892
  11.0 5.6 %collective-permute-start = (bf16[1,64,1536]{2,1,0:T(8,128)(2,1)S(1)}, bf16[1,64,1536]{2,1,0:T(8,128)(2,1)S(1)}, u32[]{:S(2)}, u32[]{:S(2)}) collective-permute-start(bf16[1,64,1536]{2,1,0:T(8,128)(2,1)S(1)} %get-tuple-element.206), channel_id=1, source_target_pairs={{0,1},{1,2},{2,3},{3,4},{4,5},{5,6},{6,7},{8,9},{9,10},{10,11},{11... | collective-permute-start | bytes 589832 | tf_op jit(solution)/shard_map/ppermute | solution.py:15
  13.4 5.4 %collective-permute-start.1 = (bf16[1,64,1536]{2,1,0:T(8,128)(2,1)S(1)}, bf16[1,64,1536]{2,1,0:T(8,128)(2,1)S(1)}, u32[]{:S(2)}, u32[]{:S(2)}) collective-permute-start(bf16[1,64,1536]{2,1,0:T(8,128)(2,1)S(1)} %get-tuple-element.207), channel_id=1, source_target_pairs={{1,0},{2,1},{3,2},{4,3},{5,4},{6,5},{7,6},{9,8},{10,9},{11,10},{12... | collective-permute-start | bytes 589832 | tf_op jit(solution)/shard_map/ppermute | solution.py:18
  41.8 1.1 copy-start.3
  142.3 4.7 %copy-start.1 = (bf16[50,4608]{1,0:T(8,128)(2,1)S(1)}, bf16[50,4608]{1,0:T(8,128)(2,1)}, u32[]{:S(2)}) copy-start(bf16[50,4608]{1,0:T(8,128)(2,1)} %param.13) | copy-start | bytes 1382404
Sparse Core Ops, SparseCore 0:
  10.0 77.5 all-gather.1
where the time goes:
time: 154 us
  matrix products  53.2 us (35%)
  waiting for transfers between devices  44.6 us (29%)
  local copies, waits for them, and re-layouts  20.1 us (13%)
  other arithmetic  16.6 us (11%)
  between operations  15.5 us (10%)
  starting transfers between devices  3.7 us (2%)
    all_gather x1, waiting for transfers between devices, per_device(): whole = lax.all_gather(stale_kv, 'patch', axis=0, tiled=True)  42.3 us
    dot_general x4, matrix products, step(): jnp.einsum('hqk,khe->hqe', expo.astype(jnp.bfloat16), values, preferred_e...  22 us
    dot_general x4, matrix products, step(): jnp.einsum('qhe,khe->hqk', query, keys, preferred_element_type=jnp.float32)  12 us
    reduce_sum x4, other arithmetic, step(): total = total * factor + jnp.sum(expo, axis=2)  10.4 us
    dot_general x1, matrix products, per_device(): projected = jnp.dot(normed, w_qkv, preferred_element_type=jnp.float32)  9.6 us
    slice x4, local copies, waits for them, and re-layouts, step(): values = part_kv[:, width:].reshape(block, heads, size)  8.41 us
    dot_general x1, matrix products, per_device(): proj = jnp.dot(attended, w_out, preferred_element_type=jnp.float32)  4.68 us
    unnamed x13, local copies, waits for them, and re-layouts  3.84 us
  transfers between devices with their start and end apart: 3, of which 2 were waited for; matrix products, arithmetic and copies ran while one was open for 17% of the time, Pallas kernels for 0%

commit v1 on v0

v1 whole, which is shorter than its diff:
```python
import functools

import jax
import jax.numpy as jnp
from jax import lax
from jax.experimental import pallas as pl
from jax.experimental.pallas import tpu as pltpu
from jax.sharding import PartitionSpec as P

HEADS = 24
GRID_W = 64
LANES = 128
GROUP = 2
CHUNK = 512


def kernel(
    count,
    timestep,
    action,
    latent,
    conv_weight,
    time_table,
    action_table,
    w_qkv,
    w_out,
    stale,
    layer_out,
    fresh,
    kv,
    wq,
    wo,
    halo,
    mixed,
    normed,
    qbd,
    acc,
    tops,
    totals,
    modulation,
    halo_send,
    halo_recv,
    own_send,
    relay_send,
    cross_send,
    recv,
    load_sem,
):
    rows, width = latent.shape
    half = rows // 2
    size = width // HEADS
    pairs = width // LANES
    chips = count // 2
    me = lax.axis_index("patch")
    core = me % 2
    chip = me // 2
    sibling = chip * 2 + (1 - core)

    def part(h):
        return pl.ds(h * half, half)

    def target(j):
        if chips == 4:
            other = chip + 1 - 2 * (chip % 2) if j == 1 else (chip + 2) % 4
        else:
            other = (chip + chips - j) % chips
        return other * 2 + core

    def send(src, role, h, sem, device):
        copy = pltpu.make_async_remote_copy(
            src_ref=src,
            dst_ref=kv.at[role - 1, part(h)],
            send_sem=sem,
            recv_sem=recv.at[role - 1, h],
            device_id={"patch": device},
            device_id_type=pl.DeviceIdType.MESH,
        )
        copy.start()
        return copy

    def arrived(role, h):
        pltpu.make_async_remote_copy(
            src_ref=kv.at[role - 1, part(h)],
            dst_ref=kv.at[role - 1, part(h)],
            send_sem=cross_send.at[0],
            recv_sem=recv.at[role - 1, h],
            device_id={"patch": sibling},
            device_id_type=pl.DeviceIdType.MESH,
        ).wait_recv()

    loads = [
        pltpu.make_async_copy(w_qkv, wq, load_sem.at[0]),
        pltpu.make_async_copy(w_out, wo, load_sem.at[1]),
    ]
    for load in loads:
        load.start()

    barrier = pltpu.get_barrier_semaphore()
    for step in range(1, count):
        pl.semaphore_signal(
            barrier,
            inc=1,
            device_id={"patch": (me + step) % count},
            device_id_type=pl.DeviceIdType.MESH,
        )
    pl.semaphore_wait(barrier, count - 1)

    edges = []
    for slot, (start, device) in enumerate(
        ((rows - GRID_W, (me + 1) % count), (0, (me + count - 1) % count))
    ):
        copy = pltpu.make_async_remote_copy(
            src_ref=latent.at[pl.ds(start, GRID_W)],
            dst_ref=halo.at[slot],
            send_sem=halo_send.at[slot],
            recv_sem=halo_recv.at[slot],
            device_id={"patch": device},
            device_id_type=pl.DeviceIdType.MESH,
        )
        copy.start()
        edges.append(copy)

    sent = []
    direct = (1, 2) if chips == 4 else tuple(range(1, chips))
    for order in range(2):
        for j in direct:
            h = order if j % 2 == 1 else 1 - order
            sent.append(send(stale.at[part(h)], 2 * j, h, own_send.at[j, h], target(j)))
        sent.append(send(stale.at[part(order)], 1, order, own_send.at[0, order], sibling))

    def relay(j, h):
        arrived(2 * j, h)
        if chips == 4 and (j, h) == (1, 0):
            sent.append(send(kv.at[1, part(0)], 6, 0, cross_send.at[0], target(2)))
        if chips == 4 and (j, h) == (2, 1):
            sent.append(send(kv.at[3, part(1)], 6, 1, cross_send.at[1], target(1)))
        sent.append(
            send(kv.at[2 * j - 1, part(h)], 2 * j + 1, h, relay_send.at[j - 1, h], sibling)
        )

    def pick(table, index):
        hot = lax.broadcasted_iota(jnp.int32, table.shape, 0) == index
        return jnp.sum(
            jnp.where(hot, table[...].astype(jnp.float32), 0.0), axis=0, keepdims=True
        )

    modulation[...] = pick(time_table, timestep[0]) + pick(action_table, action[0])

    nrows = rows // GRID_W

    def stem(r):
        def body(c, carry):
            cols = pl.ds(pl.multiple_of(c * 2 * LANES, 2 * LANES), 2 * LANES)
            taps = conv_weight[:, cols]
            lines = []
            for a in (r - 1, r, r + 1):
                if a < 0:
                    line = jnp.where(me > 0, halo[0, :, cols].astype(jnp.float32), 0.0)
                elif a >= nrows:
                    line = jnp.where(me < count - 1, halo[1, :, cols].astype(jnp.float32), 0.0)
                else:
                    line = latent[pl.ds(a * GRID_W, GRID_W), cols].astype(jnp.float32)
                lines.append(line)
            sums = []
            for b in range(3):
                total = lines[0] * taps[b : b + 1]
                total = total + lines[1] * taps[3 + b : 4 + b]
                sums.append(total + lines[2] * taps[6 + b : 7 + b])
            place = lax.broadcasted_iota(jnp.int32, sums[0].shape, 0)
            before = jnp.where(place == 0, 0.0, pltpu.roll(sums[0], 1, 0))
            after = jnp.where(place == GRID_W - 1, 0.0, pltpu.roll(sums[2], GRID_W - 1, 0))
            mixed[pl.ds(r * GRID_W, GRID_W), cols] = lines[1] + sums[1] + (before + after)
            return carry

        lax.fori_loop(0, width // (2 * LANES), body, 0)

    for r in range(1, nrows - 1):
        stem(r)
    for edge in edges:
        edge.wait_recv()
    stem(0)
    stem(nrows - 1)

    def norm(r, carry):
        span = pl.ds(pl.multiple_of(r * 32, 32), 32)
        x = mixed[span, :]
        mean = jnp.mean(x, axis=1, keepdims=True)
        centred = x - mean
        var = jnp.mean(centred * centred, axis=1, keepdims=True)
        gain = 1.0 + modulation[:, width : 2 * width]
        normed[span, :] = (
            centred * lax.rsqrt(var + 1e-06) * gain + modulation[:, :width]
        ).astype(jnp.bfloat16)
        return carry

    lax.fori_loop(0, rows // 32, norm, 0)

    loads[0].wait()
    qbd[...] = jnp.zeros_like(qbd)
    per = CHUNK // LANES

    def project(c):
        cols = pl.ds(pl.multiple_of(c * CHUNK, CHUNK), CHUNK)
        return jnp.dot(normed[...], wq[:, cols], preferred_element_type=jnp.float32)

    def queries(c, carry):
        block = project(c) * size ** (-0.5)
        for u in range(per):
            flipped = jnp.transpose(block[:, u * LANES : (u + 1) * LANES]).astype(jnp.bfloat16)
            qbd[c * per + u, :size, :rows] = flipped[:size]
            qbd[c * per + u, size:, rows:] = flipped[size:]
        return carry

    lax.fori_loop(0, width // CHUNK, queries, 0)

    def keys_values(c, carry):
        cols = pl.ds(pl.multiple_of(c * CHUNK, CHUNK), CHUNK)
        fresh[:, cols] = project(c + width // CHUNK).astype(jnp.bfloat16)
        return carry

    lax.fori_loop(0, 2 * width // CHUNK, keys_values, 0)

    def attend(read, first=False):
        def body(g, carry):
            done = []
            for u in range(GROUP):
                i = g * GROUP + u
                col = pl.multiple_of(i * LANES, LANES)
                scores = jnp.dot(
                    read(pl.ds(col, LANES)), qbd[i], preferred_element_type=jnp.float32
                )
                top = jnp.max(scores, axis=0, keepdims=True)
                if not first:
                    top = jnp.maximum(top, tops[i])
                expo = jnp.exp(scores - top)
                total = jnp.sum(expo, axis=0, keepdims=True)
                weights = expo.astype(jnp.bfloat16)
                flipped = jnp.transpose(read(pl.ds(pl.multiple_of(width + col, LANES), LANES)))
                summed = jnp.concatenate(
                    [
                        jnp.dot(
                            flipped[:size], weights[:, :rows], preferred_element_type=jnp.float32
                        ),
                        jnp.dot(
                            flipped[size:], weights[:, rows:], preferred_element_type=jnp.float32
                        ),
                    ],
                    axis=1,
                )
                if not first:
                    factor = jnp.exp(tops[i] - top)
                    total = total + totals[i] * factor
                    summed = summed + acc[i] * factor
                done.append((i, top, total, summed))
            for i, top, total, summed in done:
                tops[i] = top
                totals[i] = total
                acc[i] = summed
            return carry

        lax.fori_loop(0, pairs // GROUP, body, 0)

    def two(first, second):
        def read(cols):
            return jnp.concatenate(
                [kv[role - 1, part(h), cols] for role, h in (first, second)], axis=0
            )

        return read

    attend(lambda cols: fresh[:, cols], first=True)
    arrived(1, 0)
    arrived(1, 1)
    attend(two((1, 0), (1, 1)))
    if chips == 4:
        plan = [((1, 0), (2, 1)), ((1, 1), (2, 0)), ((3, 0), (3, 1))]
    else:
        plan = [((j, 0), (j, 1)) for j in range(1, chips)]
    for one, other in plan:
        relay(*one)
        relay(*other)
        attend(two((2 * one[0], one[1]), (2 * other[0], other[1])))
        arrived(2 * one[0] + 1, one[1])
        arrived(2 * other[0] + 1, other[1])
        attend(two((2 * one[0] + 1, one[1]), (2 * other[0] + 1, other[1])))

    def finish(i, carry):
        result = acc[i] / totals[i]
        stacked = jnp.concatenate([result[:, :rows], result[:, rows:]], axis=0)
        cols = pl.ds(pl.multiple_of(i * LANES, LANES), LANES)
        normed[:, cols] = jnp.transpose(stacked).astype(jnp.bfloat16)
        return carry

    lax.fori_loop(0, pairs, finish, 0)
    loads[1].wait()

    def output(c, carry):
        cols = pl.ds(pl.multiple_of(c * CHUNK, CHUNK), CHUNK)
        proj = jnp.dot(normed[...], wo[:, cols], preferred_element_type=jnp.float32)
        gate = modulation[:, pl.ds(pl.multiple_of(2 * width + c * CHUNK, CHUNK), CHUNK)]
        layer_out[:, cols] = (mixed[:, cols] + gate * proj).astype(jnp.bfloat16)
        return carry

    lax.fori_loop(0, width // CHUNK, output, 0)

    for copy in edges + sent:
        copy.wait_send()


def per_device(
    count, latent, conv_weight, time_table, action_table, timestep, action, w_qkv, w_out, stale_kv
):
    rows, width = latent.shape
    pairs = width // LANES
    size = width // HEADS
    chips = count // 2
    vmem = pl.BlockSpec(memory_space=pltpu.VMEM)
    smem = pl.BlockSpec(memory_space=pltpu.SMEM)
    anywhere = pl.BlockSpec(memory_space=pl.ANY)
    dma = pltpu.SemaphoreType.DMA
    return pl.pallas_call(
        functools.partial(kernel, count),
        out_shape=(
            jax.ShapeDtypeStruct((rows, width), jnp.bfloat16),
            jax.ShapeDtypeStruct((rows, 2 * width), jnp.bfloat16),
        ),
        in_specs=[smem, smem, vmem, vmem, vmem, vmem, anywhere, anywhere, anywhere],
        out_specs=(vmem, vmem),
        scratch_shapes=[
            pltpu.VMEM((count - 1, rows, 2 * width), jnp.bfloat16),
            pltpu.VMEM(w_qkv.shape, jnp.bfloat16),
            pltpu.VMEM(w_out.shape, jnp.bfloat16),
            pltpu.VMEM((2, GRID_W, width), jnp.bfloat16),
            pltpu.VMEM((rows, width), jnp.float32),
            pltpu.VMEM((rows, width), jnp.bfloat16),
            pltpu.VMEM((pairs, LANES, 2 * rows), jnp.bfloat16),
            pltpu.VMEM((pairs, size, 2 * rows), jnp.float32),
            pltpu.VMEM((pairs, 1, 2 * rows), jnp.float32),
            pltpu.VMEM((pairs, 1, 2 * rows), jnp.float32),
            pltpu.VMEM((1, 3 * width), jnp.float32),
            dma((2,)),
            dma((2,)),
            dma((chips, 2)),
            dma((chips - 1, 2)),
            dma((2,)),
            dma((count - 1, 2)),
            dma((2,)),
        ],
        compiler_params=pltpu.CompilerParams(
            collective_id=0, has_side_effects=True, vmem_limit_bytes=60 * 2**20
        ),
        cost_estimate=pl.CostEstimate(
            flops=8 * 10**9, bytes_accessed=30 * 2**20, transcendentals=13 * 10**6
        ),
    )(timestep, action, latent, conv_weight, time_table, action_table, w_qkv, w_out, stale_kv)


def solution(mesh):
    in_specs = (
        P(("frame", "patch"), None),
        P(),
        P(),
        P(),
        P("frame"),
        P("frame"),
        P(),
        P(),
        P(("frame", "patch"), None),
    )
    out_specs = (P(("frame", "patch"), None), P(("frame", "patch"), None))
    return jax.shard_map(
        functools.partial(per_device, mesh.shape["patch"]),
        mesh=mesh,
        in_specs=in_specs,
        out_specs=out_specs,
        check_vma=False,
    )
```

time: 154 us -> 81.5 us (0.53)
  Pallas kernels: 0 us -> 76 us
  matrix products: 53.2 us -> 0 us
  waiting for transfers between devices: 44.6 us -> 0 us
  local copies, waits for them, and re-layouts: 20.1 us -> 3.33 us
  other arithmetic: 16.6 us -> 0 us
  between operations: 15.5 us -> 1.94 us
  starting transfers between devices: 3.7 us -> 0 us
    pallas_call x0 -> x1, Pallas kernels: none -> 76 us  [per_device(): pl.pallas_call(functools.partial(kernel, count), out_shape=(jax.ShapeDtyp...]
    dot_general x14 -> x0, matrix products: 53.2 us -> none  [the longest x4 22 us: step(): jnp.einsum('hqk,khe->hqe', expo.astype(jnp.bfloat16), values, preferred_e...]
    all_gather x1 -> x0, waiting for transfers between devices: 42.3 us -> none  [per_device(): whole = lax.all_gather(stale_kv, 'patch', axis=0, tiled=True)]
    slice x11 -> x0, local copies, waits for them, and re-layouts: 16.1 us -> none  [the longest x4 8.41 us: step(): values = part_kv[:, width:].reshape(block, heads, size)]
    reduce_sum x7 -> x0, other arithmetic: 14.2 us -> none  [the longest x4 10.4 us: step(): total = total * factor + jnp.sum(expo, axis=2)]
    ppermute x2 -> x0, starting transfers between devices: 3.66 us -> none  [the longest x1 2.37 us: padded_2(): lax.ppermute(lax.slice_in_dim(block, block.shape[dim] - width, None, axis...]
    ppermute x2 -> x0, waiting for transfers between devices: 2.22 us -> none  [the longest x1 2.22 us: padded_2(): lax.ppermute(lax.slice_in_dim(block, 0, width, axis=dim), axis, backward)]
    convert_element_type x2 -> x0, other arithmetic: 1.94 us -> none  [the longest x1 1.59 us: per_device(): jnp.transpose(result, (1, 0, 2)).reshape(rows, width).astype(jnp.bfloat16)]
  transfers between devices with their start and end apart: 3 -> 0, of which waited for: 2 -> 0; matrix products, arithmetic and copies ran while one was open for 17% -> 0% of each run, Pallas kernels for 0% -> 0%
where the time goes in v1:
time: 81.5 us; the launch traced here: 81.3 us
  Pallas kernels  76 us (93%)
  local copies, waits for them, and re-layouts  3.33 us (4%)
  between operations  1.94 us (2%)
    pallas_call x1, Pallas kernels, per_device(): pl.pallas_call(functools.partial(kernel, count), out_shape=(jax.ShapeDtyp...  76 us
    unnamed x4, local copies, waits for them, and re-layouts  3.33 us

profile of v1, /device:TPU:0, one launch (start us, length us, event | category | flops | bytes accessed | tf_op | source)
XLA Modules:
  0.0 81.3 jit_solution(9051573280276958699)
XLA Ops:
  1.9 76.0 %shard_map.104 = (bf16[256,1536]{1,0:T(8,128)(2,1)}, bf16[256,3072]{1,0:T(8,128)(2,1)}) custom-call(s32[1]{0:T(128)S(6)} %copy.13.timestep, s32[1]{0:T(128)S(6)} %copy.14.action, bf16[256,1536]{1,0:T(8,128)(2,1)} %latent.1, f32[9,1536]{1,0:T(8,128)} %conv_weight.1, bf16[50,4608]{1,0:T(8,128)(2,1)} %time_table.1, bf16[18,4608]{1,0:T(8,128)(2,1)} %action_table.1, ...), custom_call_target="tpu_custom_call" | custom-call | flops 8000000000 | bytes 31457280 | tf_op jit(solution)/shard_map/pallas_call | solution.py:321
  78.0 0.0 copy-start
  78.0 2.2 %copy.15 = bf16[256,1536]{1,0:T(8,128)(2,1)} copy(bf16[256,1536]{1,0:T(8,128)(2,1)} %get-tuple-element.4) | data formatting | bytes 1572864
  80.2 0.0 copy-done
  80.2 1.1 %copy.16 = bf16[256,3072]{1,0:T(8,128)(2,1)} copy(bf16[256,3072]{1,0:T(8,128)(2,1)S(1)} %copy-done) | data formatting | bytes 3145728
Async XLA Ops:
  78.0 2.2 %copy-start = (bf16[256,3072]{1,0:T(8,128)(2,1)S(1)}, bf16[256,3072]{1,0:T(8,128)(2,1)}, u32[]{:S(2)}) copy-start(bf16[256,3072]{1,0:T(8,128)(2,1)} %get-tuple-element.5) | copy-start | bytes 4718596

commit v2 on v1

--- a/solution.py
+++ b/solution.py
@@ -260,29 +260,28 @@
 
         lax.fori_loop(0, pairs // GROUP, body, 0)
 
-    def two(first, second):
+    def landed(pieces):
         def read(cols):
             return jnp.concatenate(
-                [kv[role - 1, part(h), cols] for role, h in (first, second)], axis=0
+                [kv[role - 1, part(h), cols] for role, h in pieces], axis=0
             )
 
         return read
 
-    attend(lambda cols: fresh[:, cols], first=True)
     arrived(1, 0)
     arrived(1, 1)
-    attend(two((1, 0), (1, 1)))
+    beside = landed([(1, 0), (1, 1)])
+    attend(lambda cols: jnp.concatenate([fresh[:, cols], beside(cols)], axis=0), first=True)
     if chips == 4:
         plan = [((1, 0), (2, 1)), ((1, 1), (2, 0)), ((3, 0), (3, 1))]
     else:
         plan = [((j, 0), (j, 1)) for j in range(1, chips)]
-    for one, other in plan:
-        relay(*one)
-        relay(*other)
-        attend(two((2 * one[0], one[1]), (2 * other[0], other[1])))
-        arrived(2 * one[0] + 1, one[1])
-        arrived(2 * other[0] + 1, other[1])
-        attend(two((2 * one[0] + 1, one[1]), (2 * other[0] + 1, other[1])))
+    for pair in plan:
+        for j, h in pair:
+            relay(j, h)
+        for j, h in pair:
+            arrived(2 * j + 1, h)
+        attend(landed([(2 * j + c, h) for j, h in pair for c in range(2)]))
 
     def finish(i, carry):
         result = acc[i] / totals[i]

time: 81.5 us -> 81.1 us (level)
    pallas_call x1, Pallas kernels: 76 us -> 75.2 us  [per_device(): pl.pallas_call(functools.partial(kernel, count), out_shape=(jax.ShapeDtyp...]
where the time goes in v2:
time: 81.1 us; the launch traced here: 80.5 us
  Pallas kernels  75.2 us (93%)
  local copies, waits for them, and re-layouts  3.33 us (4%)
  between operations  1.94 us (2%)
    pallas_call x1, Pallas kernels, per_device(): pl.pallas_call(functools.partial(kernel, count), out_shape=(jax.ShapeDtyp...  75.2 us
    unnamed x4, local copies, waits for them, and re-layouts  3.33 us

profile of v2, /device:TPU:0, one launch (start us, length us, event | category | flops | bytes accessed | tf_op | source)
XLA Modules:
  0.0 80.5 jit_solution(9958353318230715213)
XLA Ops:
  1.9 75.2 %shard_map.104 = (bf16[256,1536]{1,0:T(8,128)(2,1)}, bf16[256,3072]{1,0:T(8,128)(2,1)}) custom-call(s32[1]{0:T(128)S(6)} %copy.13.timestep, s32[1]{0:T(128)S(6)} %copy.14.action, bf16[256,1536]{1,0:T(8,128)(2,1)} %latent.1, f32[9,1536]{1,0:T(8,128)} %conv_weight.1, bf16[50,4608]{1,0:T(8,128)(2,1)} %time_table.1, bf16[18,4608]{1,0:T(8,128)(2,1)} %action_table.1, ...), custom_call_target="tpu_custom_call" | custom-call | flops 8000000000 | bytes 31457280 | tf_op jit(solution)/shard_map/pallas_call | solution.py:320
  77.1 0.0 copy-start
  77.1 2.2 %copy.15 = bf16[256,1536]{1,0:T(8,128)(2,1)} copy(bf16[256,1536]{1,0:T(8,128)(2,1)} %get-tuple-element.4) | data formatting | bytes 1572864
  79.3 0.0 copy-done
  79.3 1.1 %copy.16 = bf16[256,3072]{1,0:T(8,128)(2,1)} copy(bf16[256,3072]{1,0:T(8,128)(2,1)S(1)} %copy-done) | data formatting | bytes 3145728
Async XLA Ops:
  77.1 2.2 %copy-start = (bf16[256,3072]{1,0:T(8,128)(2,1)S(1)}, bf16[256,3072]{1,0:T(8,128)(2,1)}, u32[]{:S(2)}) copy-start(bf16[256,3072]{1,0:T(8,128)(2,1)} %get-tuple-element.5) | copy-start | bytes 4718596

commit v3 on v2

--- a/solution.py
+++ b/solution.py
@@ -12,6 +12,81 @@
 LANES = 128
 GROUP = 2
 CHUNK = 512
+
+
+def prepare(
+    count,
+    timestep,
+    action,
+    latent,
+    conv_weight,
+    time_table,
+    action_table,
+    halo,
+    edges,
+    mixed,
+    normed,
+    modulation,
+):
+    rows, width = latent.shape
+    me = lax.axis_index("patch")
+
+    def pick(table, index):
+        hot = lax.broadcasted_iota(jnp.int32, table.shape, 0) == index
+        return jnp.sum(
+            jnp.where(hot, table[...].astype(jnp.float32), 0.0), axis=0, keepdims=True
+        )
+
+    modulation[...] = pick(time_table, timestep[0]) + pick(action_table, action[0])
+
+    nrows = rows // GRID_W
+
+    def stem(r):
+        def body(c, carry):
+            cols = pl.ds(pl.multiple_of(c * 2 * LANES, 2 * LANES), 2 * LANES)
+            taps = conv_weight[:, cols]
+            lines = []
+            for a in (r - 1, r, r + 1):
+                if a < 0:
+                    line = jnp.where(me > 0, halo[0, :, cols].astype(jnp.float32), 0.0)
+                elif a >= nrows:
+                    line = jnp.where(me < count - 1, halo[1, :, cols].astype(jnp.float32), 0.0)
+                else:
+                    line = latent[pl.ds(a * GRID_W, GRID_W), cols].astype(jnp.float32)
+                lines.append(line)
+            sums = []
+            for b in range(3):
+                total = lines[0] * taps[b : b + 1]
+                total = total + lines[1] * taps[3 + b : 4 + b]
+                sums.append(total + lines[2] * taps[6 + b : 7 + b])
+            place = lax.broadcasted_iota(jnp.int32, sums[0].shape, 0)
+            before = jnp.where(place == 0, 0.0, pltpu.roll(sums[0], 1, 0))
+            after = jnp.where(place == GRID_W - 1, 0.0, pltpu.roll(sums[2], GRID_W - 1, 0))
+            mixed[pl.ds(r * GRID_W, GRID_W), cols] = lines[1] + sums[1] + (before + after)
+            return carry
+
+        lax.fori_loop(0, width // (2 * LANES), body, 0)
+
+    for r in range(1, nrows - 1):
+        stem(r)
+    for edge in edges:
+        edge.wait_recv()
+    stem(0)
+    stem(nrows - 1)
+
+    def norm(r, carry):
+        span = pl.ds(pl.multiple_of(r * 32, 32), 32)
+        x = mixed[span, :]
+        mean = jnp.mean(x, axis=1, keepdims=True)
+        centred = x - mean
+        var = jnp.mean(centred * centred, axis=1, keepdims=True)
+        gain = 1.0 + modulation[:, width : 2 * width]
+        normed[span, :] = (
+            centred * lax.rsqrt(var + 1e-06) * gain + modulation[:, :width]
+        ).astype(jnp.bfloat16)
+        return carry
+
+    lax.fori_loop(0, rows // 32, norm, 0)
 
 
 def kernel(
@@ -138,62 +213,10 @@
             send(kv.at[2 * j - 1, part(h)], 2 * j + 1, h, relay_send.at[j - 1, h], sibling)
         )
 
-    def pick(table, index):
-        hot = lax.broadcasted_iota(jnp.int32, table.shape, 0) == index
-        return jnp.sum(
-            jnp.where(hot, table[...].astype(jnp.float32), 0.0), axis=0, keepdims=True
-        )
-
-    modulation[...] = pick(time_table, timestep[0]) + pick(action_table, action[0])
-
-    nrows = rows // GRID_W
-
-    def stem(r):
-        def body(c, carry):
-            cols = pl.ds(pl.multiple_of(c * 2 * LANES, 2 * LANES), 2 * LANES)
-            taps = conv_weight[:, cols]
-            lines = []
-            for a in (r - 1, r, r + 1):
-                if a < 0:
-                    line = jnp.where(me > 0, halo[0, :, cols].astype(jnp.float32), 0.0)
-                elif a >= nrows:
-                    line = jnp.where(me < count - 1, halo[1, :, cols].astype(jnp.float32), 0.0)
-                else:
-                    line = latent[pl.ds(a * GRID_W, GRID_W), cols].astype(jnp.float32)
-                lines.append(line)
-            sums = []
-            for b in range(3):
-                total = lines[0] * taps[b : b + 1]
-                total = total + lines[1] * taps[3 + b : 4 + b]
-                sums.append(total + lines[2] * taps[6 + b : 7 + b])
-            place = lax.broadcasted_iota(jnp.int32, sums[0].shape, 0)
-            before = jnp.where(place == 0, 0.0, pltpu.roll(sums[0], 1, 0))
-            after = jnp.where(place == GRID_W - 1, 0.0, pltpu.roll(sums[2], GRID_W - 1, 0))
-            mixed[pl.ds(r * GRID_W, GRID_W), cols] = lines[1] + sums[1] + (before + after)
-            return carry
-
-        lax.fori_loop(0, width // (2 * LANES), body, 0)
-
-    for r in range(1, nrows - 1):
-        stem(r)
-    for edge in edges:
-        edge.wait_recv()
-    stem(0)
-    stem(nrows - 1)
-
-    def norm(r, carry):
-        span = pl.ds(pl.multiple_of(r * 32, 32), 32)
-        x = mixed[span, :]
-        mean = jnp.mean(x, axis=1, keepdims=True)
-        centred = x - mean
-        var = jnp.mean(centred * centred, axis=1, keepdims=True)
-        gain = 1.0 + modulation[:, width : 2 * width]
-        normed[span, :] = (
-            centred * lax.rsqrt(var + 1e-06) * gain + modulation[:, :width]
-        ).astype(jnp.bfloat16)
-        return carry
-
-    lax.fori_loop(0, rows // 32, norm, 0)
+    prepare(
+        count, timestep, action, latent, conv_weight, time_table, action_table,
+        halo, edges, mixed, normed, modulation,
+    )
 
     loads[0].wait()
     qbd[...] = jnp.zeros_like(qbd)
@@ -306,6 +329,333 @@
         copy.wait_send()
 
 
+def remote(src, dst, send_sem, recv_sem, device):
+    return pltpu.make_async_remote_copy(
+        src_ref=src,
+        dst_ref=dst,
+        send_sem=send_sem,
+        recv_sem=recv_sem,
+        device_id={"patch": device},
+        device_id_type=pl.DeviceIdType.MESH,
+    )
+
+
+def fold(state, keys, values, query, size, rows):
+    scores = jnp.dot(keys, query, preferred_element_type=jnp.float32)
+    top = jnp.max(scores, axis=0, keepdims=True)
+    if state is not None:
+        top = jnp.maximum(top, state[0])
+    expo = jnp.exp(scores - top)
+    total = jnp.sum(expo, axis=0, keepdims=True)
+    weights = expo.astype(jnp.bfloat16)
+    flipped = jnp.transpose(values)
+    summed = jnp.concatenate(
+        [
+            jnp.dot(flipped[:size], weights[:, :rows], preferred_element_type=jnp.float32),
+            jnp.dot(flipped[size:], weights[:, rows:], preferred_element_type=jnp.float32),
+        ],
+        axis=1,
+    )
+    if state is not None:
+        factor = jnp.exp(state[0] - top)
+        total = total + state[1] * factor
+        summed = summed + state[2] * factor
+    return top, total, summed
+
+
+def blocked(flat, size, rows):
+    zero = jnp.zeros((size, rows), flat.dtype)
+    return jnp.concatenate(
+        [
+            jnp.concatenate([flat[:size], zero], axis=1),
+            jnp.concatenate([zero, flat[size:]], axis=1),
+        ],
+        axis=0,
+    )
+
+
+def spread(
+    count,
+    timestep,
+    action,
+    latent,
+    conv_weight,
+    time_table,
+    action_table,
+    w_qkv,
+    w_out,
+    stale,
+    layer_out,
+    fresh,
+    kv,
+    wq,
+    wo,
+    halo,
+    mixed,
+    normed,
+    flat,
+    asked,
+    done,
+    done_stats,
+    back,
+    back_stats,
+    acc,
+    tops,
+    totals,
+    modulation,
+    halo_send,
+    halo_recv,
+    kv_send,
+    kv_recv,
+    relay_send,
+    relay_recv,
+    ask_send,
+    ask_recv,
+    back_send,
+    back_recv,
+    load_sem,
+):
+    rows, width = latent.shape
+    size = width // HEADS
+    pairs = width // LANES
+    chips = count // 2
+    share = width // chips
+    mine = pairs // chips
+    me = lax.axis_index("patch")
+    core = me % 2
+    chip = me // 2
+    sibling = chip * 2 + (1 - core)
+
+    def target(j):
+        if chips == 4:
+            return (chip, chip + 1 - 2 * (chip % 2), (chip + 2) % 4, 3 - chip)[j]
+        return (chip + chips - j) % chips
+
+    def source(j):
+        if chips == 4:
+            return target(j)
+        return (chip + j) % chips
+
+    loads = [
+        pltpu.make_async_copy(w_qkv, wq, load_sem.at[0]),
+        pltpu.make_async_copy(w_out, wo, load_sem.at[1]),
+    ]
+    for load in loads:
+        load.start()
+
+    barrier = pltpu.get_barrier_semaphore()
+    for step in range(1, count):
+        pl.semaphore_signal(
+            barrier,
+            inc=1,
+            device_id={"patch": (me + step) % count},
+            device_id_type=pl.DeviceIdType.MESH,
+        )
+    pl.semaphore_wait(barrier, count - 1)
+
+    edges = []
+    for slot, (start, device) in enumerate(
+        ((rows - GRID_W, (me + 1) % count), (0, (me + count - 1) % count))
+    ):
+        copy = remote(
+            latent.at[pl.ds(start, GRID_W)],
+            halo.at[slot],
+            halo_send.at[slot],
+            halo_recv.at[slot],
+            device,
+        )
+        copy.start()
+        edges.append(copy)
+
+    sent = []
+    arriving = {}
+
+    def piece(owner, side):
+        start = pl.multiple_of(side * width + owner * share, LANES)
+        return stale.at[:, pl.ds(start, share)]
+
+    for side in range(2):
+        for j in list(range(chips - 1, 0, -1)) + [0]:
+            copy = remote(
+                piece(target(j), side),
+                kv.at[2 * j if j else 1, :, pl.ds(side * share, share)],
+                kv_send.at[j, side],
+                kv_recv.at[j, side],
+                target(j) * 2 + core if j else sibling,
+            )
+            copy.start()
+            sent.append(copy)
+            arriving[j, side] = copy
+        load = pltpu.make_async_copy(
+            piece(chip, side), kv.at[0, :, pl.ds(side * share, share)], load_sem.at[2 + side]
+        )
+        load.start()
+        loads.append(load)
+
+    prepare(
+        count, timestep, action, latent, conv_weight, time_table, action_table,
+        halo, edges, mixed, normed, modulation,
+    )
+
+    loads[0].wait()
+    per = CHUNK // LANES
+
+    def project(c):
+        cols = pl.ds(pl.multiple_of(c * CHUNK, CHUNK), CHUNK)
+        return jnp.dot(normed[...], wq[:, cols], preferred_element_type=jnp.float32)
+
+    def queries(c, carry):
+        block = project(c) * size ** (-0.5)
+        for u in range(per):
+            flat[c * per + u] = jnp.transpose(block[:, u * LANES : (u + 1) * LANES]).astype(
+                jnp.bfloat16
+            )
+        return carry
+
+    lax.fori_loop(0, width // CHUNK, queries, 0)
+
+    asking = []
+    for j in range(1, chips):
+        copy = remote(
+            flat.at[pl.ds(target(j) * mine, mine)],
+            asked.at[j - 1],
+            ask_send.at[j - 1],
+            ask_recv.at[j - 1],
+            target(j) * 2 + core,
+        )
+        copy.start()
+        sent.append(copy)
+        asking.append(copy)
+
+    def keys_values(c, carry):
+        cols = pl.ds(pl.multiple_of(c * CHUNK, CHUNK), CHUNK)
+        fresh[:, cols] = project(c + width // CHUNK).astype(jnp.bfloat16)
+        return carry
+
+    lax.fori_loop(0, width // CHUNK, keys_values, 0)
+
+    relays = []
+    for j in range(1, chips):
+        arriving[j, 0].wait_recv()
+        arriving[j, 1].wait_recv()
+        copy = remote(
+            kv.at[2 * j], kv.at[2 * j + 1], relay_send.at[j - 1], relay_recv.at[j - 1], sibling
+        )
+        copy.start()
+        sent.append(copy)
+        relays.append(copy)
+
+    lax.fori_loop(width // CHUNK, 2 * width // CHUNK, keys_values, 0)
+
+    loads[2].wait()
+    loads[3].wait()
+    arriving[0, 0].wait_recv()
+    arriving[0, 1].wait_recv()
+    for copy in relays:
+        copy.wait_recv()
+
+    def serve(j):
+        slots = [slot for slot in range(count) if slot != 2 * j]
+        chunks = [slots[:2], slots[2:4], slots[4:]]
+
+        def body(i, carry):
+            col = pl.multiple_of(i * LANES, LANES)
+            here, there = pl.ds(col, LANES), pl.ds(pl.multiple_of(share + col, LANES), LANES)
+            query = blocked(flat[chip * mine + i] if j == 0 else asked[j - 1, i], size, rows)
+            state = None
+            for chunk in chunks:
+                keys = jnp.concatenate([kv[slot, :, here] for slot in chunk], axis=0)
+                values = jnp.concatenate([kv[slot, :, there] for slot in chunk], axis=0)
+                state = fold(state, keys, values, query, size, rows)
+            top, total, summed = state
+            result = (summed / total).astype(jnp.bfloat16)
+            if j == 0:
+                back[0, i] = result
+                back_stats[0, pl.ds(i, 1), :] = top
+                back_stats[0, pl.ds(mine + i, 1), :] = total
+            else:
+                done[j - 1, i] = result
+                done_stats[j - 1, pl.ds(i, 1), :] = top
+                done_stats[j - 1, pl.ds(mine + i, 1), :] = total
+            return carry
+
+        lax.fori_loop(0, mine, body, 0)
+
+    serve(0)
+    returning = []
+    for j in range(chips - 1, 0, -1):
+        asking[j - 1].wait_recv()
+        serve(j)
+        for n, (src, dst) in enumerate(((done, back), (done_stats, back_stats))):
+            copy = remote(
+                src.at[j - 1],
+                dst.at[j],
+                back_send.at[j - 1, n],
+                back_recv.at[j - 1, n],
+                source(j) * 2 + core,
+            )
+            copy.start()
+            sent.append(copy)
+            returning.append(copy)
+
+    def local(g, carry):
+        found = []
+        for u in range(GROUP):
+            i = g * GROUP + u
+            col = pl.multiple_of(i * LANES, LANES)
+            found.append(
+                fold(
+                    None,
+                    fresh[:, pl.ds(col, LANES)],
+                    fresh[:, pl.ds(pl.multiple_of(width + col, LANES), LANES)],
+                    blocked(flat[i], size, rows),
+                    size,
+                    rows,
+                )
+            )
+        for u in range(GROUP):
+            i = g * GROUP + u
+            tops[i], totals[i], acc[i] = found[u]
+        return carry
+
+    lax.fori_loop(0, pairs // GROUP, local, 0)
+
+    def merge(j):
+        def body(i, carry):
+            g = target(j) * mine + i
+            there = back_stats[j, pl.ds(i, 1), :]
+            top = jnp.maximum(tops[g], there)
+            one = jnp.exp(tops[g] - top)
+            other = jnp.exp(there - top) * back_stats[j, pl.ds(mine + i, 1), :]
+            total = totals[g] * one + other
+            result = (acc[g] * one + back[j, i].astype(jnp.float32) * other) / total
+            stacked = jnp.concatenate([result[:, :rows], result[:, rows:]], axis=0)
+            cols = pl.ds(pl.multiple_of(g * LANES, LANES), LANES)
+            normed[:, cols] = jnp.transpose(stacked).astype(jnp.bfloat16)
+            return carry
+
+        lax.fori_loop(0, mine, body, 0)
+
+    merge(0)
+    for j in range(chips - 1, 0, -1):
+        for copy in returning[2 * (chips - 1 - j) : 2 * (chips - j)]:
+            copy.wait_recv()
+        merge(j)
+    loads[1].wait()
+
+    def output(c, carry):
+        cols = pl.ds(pl.multiple_of(c * CHUNK, CHUNK), CHUNK)
+        proj = jnp.dot(normed[...], wo[:, cols], preferred_element_type=jnp.float32)
+        gate = modulation[:, pl.ds(pl.multiple_of(2 * width + c * CHUNK, CHUNK), CHUNK)]
+        layer_out[:, cols] = (mixed[:, cols] + gate * proj).astype(jnp.bfloat16)
+        return carry
+
+    lax.fori_loop(0, width // CHUNK, output, 0)
+
+    for copy in edges + sent:
+        copy.wait_send()
+
+
 def per_device(
     count, latent, conv_weight, time_table, action_table, timestep, action, w_qkv, w_out, stale_kv
 ):
@@ -317,34 +667,66 @@
     smem = pl.BlockSpec(memory_space=pltpu.SMEM)
     anywhere = pl.BlockSpec(memory_space=pl.ANY)
     dma = pltpu.SemaphoreType.DMA
+    front = [
+        pltpu.VMEM(w_qkv.shape, jnp.bfloat16),
+        pltpu.VMEM(w_out.shape, jnp.bfloat16),
+        pltpu.VMEM((2, GRID_W, width), jnp.bfloat16),
+        pltpu.VMEM((rows, width), jnp.float32),
+        pltpu.VMEM((rows, width), jnp.bfloat16),
+    ]
+    state = [
+        pltpu.VMEM((pairs, size, 2 * rows), jnp.float32),
+        pltpu.VMEM((pairs, 1, 2 * rows), jnp.float32),
+        pltpu.VMEM((pairs, 1, 2 * rows), jnp.float32),
+        pltpu.VMEM((1, 3 * width), jnp.float32),
+        dma((2,)),
+        dma((2,)),
+        dma((chips, 2)),
+    ]
+    if pairs % chips == 0 and width % (chips * LANES) == 0:
+        body = spread
+        mine = pairs // chips
+        lines = 8 * pl.cdiv(2 * mine, 8)
+        scratch = [
+            pltpu.VMEM((count, rows, 2 * width // chips), jnp.bfloat16),
+            *front,
+            pltpu.VMEM((pairs, LANES, rows), jnp.bfloat16),
+            pltpu.VMEM((chips - 1, mine, LANES, rows), jnp.bfloat16),
+            pltpu.VMEM((chips - 1, mine, size, 2 * rows), jnp.bfloat16),
+            pltpu.VMEM((chips - 1, lines, 2 * rows), jnp.float32),
+            pltpu.VMEM((chips, mine, size, 2 * rows), jnp.bfloat16),
+            pltpu.VMEM((chips, lines, 2 * rows), jnp.float32),
+            *state,
+            dma((chips, 2)),
+            dma((chips - 1,)),
+            dma((chips - 1,)),
+            dma((chips - 1,)),
+            dma((chips - 1,)),
+            dma((chips - 1, 2)),
+            dma((chips - 1, 2)),
+            dma((4,)),
+        ]
+    else:
+        body = kernel
+        scratch = [
+            pltpu.VMEM((count - 1, rows, 2 * width), jnp.bfloat16),
+            *front,
+            pltpu.VMEM((pairs, LANES, 2 * rows), jnp.bfloat16),
+            *state,
+            dma((chips - 1, 2)),
+            dma((2,)),
+            dma((count - 1, 2)),
+            dma((2,)),
+        ]
     return pl.pallas_call(
-        functools.partial(kernel, count),
+        functools.partial(body, count),
         out_shape=(
             jax.ShapeDtypeStruct((rows, width), jnp.bfloat16),
             jax.ShapeDtypeStruct((rows, 2 * width), jnp.bfloat16),
         ),
         in_specs=[smem, smem, vmem, vmem, vmem, vmem, anywhere, anywhere, anywhere],
         out_specs=(vmem, vmem),
-        scratch_shapes=[
-            pltpu.VMEM((count - 1, rows, 2 * width), jnp.bfloat16),
-            pltpu.VMEM(w_qkv.shape, jnp.bfloat16),
-            pltpu.VMEM(w_out.shape, jnp.bfloat16),
-            pltpu.VMEM((2, GRID_W, width), jnp.bfloat16),
-            pltpu.VMEM((rows, width), jnp.float32),
-            pltpu.VMEM((rows, width), jnp.bfloat16),
-            pltpu.VMEM((pairs, LANES, 2 * rows), jnp.bfloat16),
-            pltpu.VMEM((pairs, size, 2 * rows), jnp.float32),
-            pltpu.VMEM((pairs, 1, 2 * rows), jnp.float32),
-            pltpu.VMEM((pairs, 1, 2 * rows), jnp.float32),
-            pltpu.VMEM((1, 3 * width), jnp.float32),
-            dma((2,)),
-            dma((2,)),
-            dma((chips, 2)),
-            dma((chips - 1, 2)),
-            dma((2,)),
-            dma((count - 1, 2)),
-            dma((2,)),
-        ],
+        scratch_shapes=scratch,
         compiler_params=pltpu.CompilerParams(
             collective_id=0, has_side_effects=True, vmem_limit_bytes=60 * 2**20
         ),

time: 81.1 us -> 69.2 us (0.85)
  Pallas kernels: 75.2 us -> 63.8 us
    pallas_call x1, Pallas kernels: 75.2 us -> 63.8 us  [per_device(): pl.pallas_call(functools.partial(body, count), out_shape=(jax.ShapeDtypeS...]
where the time goes in v3:
time: 69.2 us; the launch traced here: 69 us
  Pallas kernels  63.8 us (92%)
  local copies, waits for them, and re-layouts  3.33 us (5%)
  between operations  1.94 us (3%)
    pallas_call x1, Pallas kernels, per_device(): pl.pallas_call(functools.partial(body, count), out_shape=(jax.ShapeDtypeS...  63.8 us
    unnamed x4, local copies, waits for them, and re-layouts  3.33 us

profile of v3, /device:TPU:0, one launch (start us, length us, event | category | flops | bytes accessed | tf_op | source)
XLA Modules:
  0.0 69.0 jit_solution(8623376851195775522)
XLA Ops:
  1.9 63.8 %shard_map.104 = (bf16[256,1536]{1,0:T(8,128)(2,1)}, bf16[256,3072]{1,0:T(8,128)(2,1)}) custom-call(s32[1]{0:T(128)S(6)} %copy.13.timestep, s32[1]{0:T(128)S(6)} %copy.14.action, bf16[256,1536]{1,0:T(8,128)(2,1)} %latent.1, f32[9,1536]{1,0:T(8,128)} %conv_weight.1, bf16[50,4608]{1,0:T(8,128)(2,1)} %time_table.1, bf16[18,4608]{1,0:T(8,128)(2,1)} %action_table.1, ...), custom_call_target="tpu_custom_call" | custom-call | flops 8000000000 | bytes 31457280 | tf_op jit(solution)/shard_map/pallas_call | solution.py:721
  65.7 0.0 copy-start
  65.7 2.2 %copy.15 = bf16[256,1536]{1,0:T(8,128)(2,1)} copy(bf16[256,1536]{1,0:T(8,128)(2,1)} %get-tuple-element.4) | data formatting | bytes 1572864
  67.9 0.0 copy-done
  67.9 1.1 %copy.16 = bf16[256,3072]{1,0:T(8,128)(2,1)} copy(bf16[256,3072]{1,0:T(8,128)(2,1)S(1)} %copy-done) | data formatting | bytes 3145728
Async XLA Ops:
  65.7 2.2 %copy-start = (bf16[256,3072]{1,0:T(8,128)(2,1)S(1)}, bf16[256,3072]{1,0:T(8,128)(2,1)}, u32[]{:S(2)}) copy-start(bf16[256,3072]{1,0:T(8,128)(2,1)} %get-tuple-element.5) | copy-start | bytes 4718596

commit v4 on v3

--- a/solution.py
+++ b/solution.py
@@ -11,6 +11,7 @@
 GRID_W = 64
 LANES = 128
 GROUP = 2
+MANY = 4
 CHUNK = 512
 
 
@@ -340,15 +341,13 @@
     )
 
 
-def fold(state, keys, values, query, size, rows):
-    scores = jnp.dot(keys, query, preferred_element_type=jnp.float32)
+def fold(state, scores, flipped, size, rows):
     top = jnp.max(scores, axis=0, keepdims=True)
     if state is not None:
         top = jnp.maximum(top, state[0])
     expo = jnp.exp(scores - top)
     total = jnp.sum(expo, axis=0, keepdims=True)
     weights = expo.astype(jnp.bfloat16)
-    flipped = jnp.transpose(values)
     summed = jnp.concatenate(
         [
             jnp.dot(flipped[:size], weights[:, :rows], preferred_element_type=jnp.float32),
@@ -361,6 +360,20 @@
         total = total + state[1] * factor
         summed = summed + state[2] * factor
     return top, total, summed
+
+
+def pipeline(tasks, size, rows):
+    states = {}
+    waiting = None
+    for task in tasks + [None]:
+        ahead = None
+        if task is not None:
+            ahead = jnp.dot(task[1](), task[3], preferred_element_type=jnp.float32)
+        if waiting is not None:
+            (stream, _, values, _), scores = waiting
+            states[stream] = fold(states.get(stream), scores, values(), size, rows)
+        waiting = (task, ahead)
+    return states
 
 
 def blocked(flat, size, rows):
@@ -394,6 +407,7 @@
     mixed,
     normed,
     flat,
+    turned,
     asked,
     done,
     done_stats,
@@ -532,7 +546,30 @@
         fresh[:, cols] = project(c + width // CHUNK).astype(jnp.bfloat16)
         return carry
 
-    lax.fori_loop(0, width // CHUNK, keys_values, 0)
+    lax.fori_loop(0, 2 * width // CHUNK, keys_values, 0)
+
+    def local(g, carry):
+        def read(start):
+            return fresh[:, pl.ds(pl.multiple_of(start, LANES), LANES)]
+
+        def task(u):
+            i = g * MANY + u
+            return (
+                u,
+                lambda: read(i * LANES),
+                lambda: jnp.transpose(read(width + i * LANES)),
+                blocked(flat[i], size, rows),
+            )
+
+        found = pipeline([task(u) for u in range(MANY)], size, rows)
+        for u in range(MANY):
+            i = g * MANY + u
+            tops[i], totals[i], acc[i] = found[u]
+        return carry
+
+    early = pairs // MANY - 1
+
+    lax.fori_loop(0, early, local, 0)
 
     relays = []
     for j in range(1, chips):
@@ -545,41 +582,53 @@
         sent.append(copy)
         relays.append(copy)
 
-    lax.fori_loop(width // CHUNK, 2 * width // CHUNK, keys_values, 0)
+    def turn(slot, carry):
+        for i in range(mine):
+            turned[i, :, pl.ds(pl.multiple_of(slot * rows, rows), rows)] = jnp.transpose(
+                kv[slot, :, pl.ds(share + i * LANES, LANES)]
+            )
+        return carry
 
     loads[2].wait()
     loads[3].wait()
     arriving[0, 0].wait_recv()
     arriving[0, 1].wait_recv()
+    turn(1, 0)
+    lax.fori_loop(0, chips, lambda n, carry: turn(2 * n, carry), 0)
     for copy in relays:
         copy.wait_recv()
+    lax.fori_loop(1, chips, lambda n, carry: turn(2 * n + 1, carry), 0)
 
     def serve(j):
         slots = [slot for slot in range(count) if slot != 2 * j]
-        chunks = [slots[:2], slots[2:4], slots[4:]]
-
-        def body(i, carry):
-            col = pl.multiple_of(i * LANES, LANES)
-            here, there = pl.ds(col, LANES), pl.ds(pl.multiple_of(share + col, LANES), LANES)
-            query = blocked(flat[chip * mine + i] if j == 0 else asked[j - 1, i], size, rows)
-            state = None
-            for chunk in chunks:
-                keys = jnp.concatenate([kv[slot, :, here] for slot in chunk], axis=0)
-                values = jnp.concatenate([kv[slot, :, there] for slot in chunk], axis=0)
-                state = fold(state, keys, values, query, size, rows)
-            top, total, summed = state
+        chunks = [slots[n : n + 2] for n in range(0, count - 4, 2)] + [slots[count - 4 :]]
+        queries = [
+            blocked(flat[chip * mine + i] if j == 0 else asked[j - 1, i], size, rows)
+            for i in range(mine)
+        ]
+
+        def keys(chunk, i):
+            cols = pl.ds(i * LANES, LANES)
+            return lambda: jnp.concatenate([kv[slot, :, cols] for slot in chunk], axis=0)
+
+        def values(chunk, i):
+            return lambda: jnp.concatenate(
+                [turned[i, :, pl.ds(slot * rows, rows)] for slot in chunk], axis=1
+            )
+
+        tasks = [
+            (i, keys(chunk, i), values(chunk, i), queries[i])
+            for chunk in chunks
+            for i in range(mine)
+        ]
+        for i, (top, total, summed) in pipeline(tasks, size, rows).items():
             result = (summed / total).astype(jnp.bfloat16)
-            if j == 0:
-                back[0, i] = result
-                back_stats[0, pl.ds(i, 1), :] = top
-                back_stats[0, pl.ds(mine + i, 1), :] = total
-            else:
-                done[j - 1, i] = result
-                done_stats[j - 1, pl.ds(i, 1), :] = top
-                done_stats[j - 1, pl.ds(mine + i, 1), :] = total
-            return carry
-
-        lax.fori_loop(0, mine, body, 0)
+            place, stats = (back.at[0], back_stats.at[0])
+            if j > 0:
+                place, stats = (done.at[j - 1], done_stats.at[j - 1])
+            place[i] = result
+            stats[i : i + 1, :] = top
+            stats[mine + i : mine + i + 1, :] = total
 
     serve(0)
     returning = []
@@ -598,27 +647,7 @@
             sent.append(copy)
             returning.append(copy)
 
-    def local(g, carry):
-        found = []
-        for u in range(GROUP):
-            i = g * GROUP + u
-            col = pl.multiple_of(i * LANES, LANES)
-            found.append(
-                fold(
-                    None,
-                    fresh[:, pl.ds(col, LANES)],
-                    fresh[:, pl.ds(pl.multiple_of(width + col, LANES), LANES)],
-                    blocked(flat[i], size, rows),
-                    size,
-                    rows,
-                )
-            )
-        for u in range(GROUP):
-            i = g * GROUP + u
-            tops[i], totals[i], acc[i] = found[u]
-        return carry
-
-    lax.fori_loop(0, pairs // GROUP, local, 0)
+    lax.fori_loop(early, pairs // MANY, local, 0)
 
     def merge(j):
         def body(i, carry):
@@ -691,6 +720,7 @@
             pltpu.VMEM((count, rows, 2 * width // chips), jnp.bfloat16),
             *front,
             pltpu.VMEM((pairs, LANES, rows), jnp.bfloat16),
+            pltpu.VMEM((mine, LANES, count * rows), jnp.bfloat16),
             pltpu.VMEM((chips - 1, mine, LANES, rows), jnp.bfloat16),
             pltpu.VMEM((chips - 1, mine, size, 2 * rows), jnp.bfloat16),
             pltpu.VMEM((chips - 1, lines, 2 * rows), jnp.float32),

time: 69.2 us -> 64.2 us (0.928)
  Pallas kernels: 63.8 us -> 58.7 us
    pallas_call x1, Pallas kernels: 63.8 us -> 58.7 us  [per_device(): pl.pallas_call(functools.partial(body, count), out_shape=(jax.ShapeDtypeS...]
where the time goes in v4:
time: 64.2 us; the launch traced here: 64 us
  Pallas kernels  58.7 us (91%)
  local copies, waits for them, and re-layouts  3.33 us (5%)
  between operations  1.94 us (3%)
    pallas_call x1, Pallas kernels, per_device(): pl.pallas_call(functools.partial(body, count), out_shape=(jax.ShapeDtypeS...  58.7 us
    unnamed x4, local copies, waits for them, and re-layouts  3.33 us

profile of v4, /device:TPU:0, one launch (start us, length us, event | category | flops | bytes accessed | tf_op | source)
XLA Modules:
  0.0 64.0 jit_solution(17393154543603293870)
XLA Ops:
  1.9 58.7 %shard_map.104 = (bf16[256,1536]{1,0:T(8,128)(2,1)}, bf16[256,3072]{1,0:T(8,128)(2,1)}) custom-call(s32[1]{0:T(128)S(6)} %copy.13.timestep, s32[1]{0:T(128)S(6)} %copy.14.action, bf16[256,1536]{1,0:T(8,128)(2,1)} %latent.1, f32[9,1536]{1,0:T(8,128)} %conv_weight.1, bf16[50,4608]{1,0:T(8,128)(2,1)} %time_table.1, bf16[18,4608]{1,0:T(8,128)(2,1)} %action_table.1, ...), custom_call_target="tpu_custom_call" | custom-call | flops 8000000000 | bytes 31457280 | tf_op jit(solution)/shard_map/pallas_call | solution.py:751
  60.7 0.0 copy-start
  60.7 2.2 %copy.15 = bf16[256,1536]{1,0:T(8,128)(2,1)} copy(bf16[256,1536]{1,0:T(8,128)(2,1)} %get-tuple-element.4) | data formatting | bytes 1572864
  62.9 0.0 copy-done
  62.9 1.1 %copy.16 = bf16[256,3072]{1,0:T(8,128)(2,1)} copy(bf16[256,3072]{1,0:T(8,128)(2,1)S(1)} %copy-done) | data formatting | bytes 3145728
Async XLA Ops:
  60.7 2.2 %copy-start = (bf16[256,3072]{1,0:T(8,128)(2,1)S(1)}, bf16[256,3072]{1,0:T(8,128)(2,1)}, u32[]{:S(2)}) copy-start(bf16[256,3072]{1,0:T(8,128)(2,1)} %get-tuple-element.5) | copy-start | bytes 4718596

commit v5 on v4

--- a/solution.py
+++ b/solution.py
@@ -488,8 +488,8 @@
         start = pl.multiple_of(side * width + owner * share, LANES)
         return stale.at[:, pl.ds(start, share)]
 
-    for side in range(2):
-        for j in list(range(chips - 1, 0, -1)) + [0]:
+    for j in range(chips):
+        for side in range(2):
             copy = remote(
                 piece(target(j), side),
                 kv.at[2 * j if j else 1, :, pl.ds(side * share, share)],
@@ -500,6 +500,7 @@
             copy.start()
             sent.append(copy)
             arriving[j, side] = copy
+    for side in range(2):
         load = pltpu.make_async_copy(
             piece(chip, side), kv.at[0, :, pl.ds(side * share, share)], load_sem.at[2 + side]
         )
@@ -528,8 +529,8 @@
 
     lax.fori_loop(0, width // CHUNK, queries, 0)
 
-    asking = []
-    for j in range(1, chips):
+    asking = {}
+    for j in range(chips - 1, 0, -1):
         copy = remote(
             flat.at[pl.ds(target(j) * mine, mine)],
             asked.at[j - 1],
@@ -539,7 +540,7 @@
         )
         copy.start()
         sent.append(copy)
-        asking.append(copy)
+        asking[j] = copy
 
     def keys_values(c, carry):
         cols = pl.ds(pl.multiple_of(c * CHUNK, CHUNK), CHUNK)
@@ -571,45 +572,57 @@
 
     lax.fori_loop(0, early, local, 0)
 
-    relays = []
-    for j in range(1, chips):
-        arriving[j, 0].wait_recv()
-        arriving[j, 1].wait_recv()
-        copy = remote(
-            kv.at[2 * j], kv.at[2 * j + 1], relay_send.at[j - 1], relay_recv.at[j - 1], sibling
-        )
-        copy.start()
-        sent.append(copy)
-        relays.append(copy)
-
-    def turn(slot, carry):
-        for i in range(mine):
-            turned[i, :, pl.ds(pl.multiple_of(slot * rows, rows), rows)] = jnp.transpose(
-                kv[slot, :, pl.ds(share + i * LANES, LANES)]
-            )
-        return carry
-
-    loads[2].wait()
-    loads[3].wait()
-    arriving[0, 0].wait_recv()
-    arriving[0, 1].wait_recv()
-    turn(1, 0)
-    lax.fori_loop(0, chips, lambda n, carry: turn(2 * n, carry), 0)
-    for copy in relays:
-        copy.wait_recv()
-    lax.fori_loop(1, chips, lambda n, carry: turn(2 * n + 1, carry), 0)
+    relays = {}
+
+    def ready(chunk):
+        for slot in chunk:
+            j = slot // 2
+            if slot == 0:
+                loads[2].wait()
+                loads[3].wait()
+            elif slot == 1:
+                arriving[0, 0].wait_recv()
+                arriving[0, 1].wait_recv()
+            elif slot % 2 == 0:
+                arriving[j, 0].wait_recv()
+                arriving[j, 1].wait_recv()
+                relays[j] = remote(
+                    kv.at[slot],
+                    kv.at[slot + 1],
+                    relay_send.at[j - 1],
+                    relay_recv.at[j - 1],
+                    sibling,
+                )
+                relays[j].start()
+                sent.append(relays[j])
+            else:
+                relays[j].wait_recv()
+        for slot in chunk:
+            for i in range(mine):
+                turned[i, :, pl.ds(slot * rows, rows)] = jnp.transpose(
+                    kv[slot, :, pl.ds(share + i * LANES, LANES)]
+                )
 
     def serve(j):
         slots = [slot for slot in range(count) if slot != 2 * j]
         chunks = [slots[n : n + 2] for n in range(0, count - 4, 2)] + [slots[count - 4 :]]
+        if j == 0:
+            near = [2 * n for n in range(1, chips - 1)]
+            chunks = [[1] + near, [slot + 1 for slot in near], [count - 2], [count - 1]]
+            chunks = [chunk for chunk in chunks if chunk]
         queries = [
             blocked(flat[chip * mine + i] if j == 0 else asked[j - 1, i], size, rows)
             for i in range(mine)
         ]
 
         def keys(chunk, i):
-            cols = pl.ds(i * LANES, LANES)
-            return lambda: jnp.concatenate([kv[slot, :, cols] for slot in chunk], axis=0)
+            def read():
+                if j == 0 and i == 0:
+                    ready(chunk)
+                cols = pl.ds(i * LANES, LANES)
+                return jnp.concatenate([kv[slot, :, cols] for slot in chunk], axis=0)
+
+            return read
 
         def values(chunk, i):
             return lambda: jnp.concatenate(
@@ -631,9 +644,10 @@
             stats[mine + i : mine + i + 1, :] = total
 
     serve(0)
+    ready([0])
     returning = []
     for j in range(chips - 1, 0, -1):
-        asking[j - 1].wait_recv()
+        asking[j].wait_recv()
         serve(j)
         for n, (src, dst) in enumerate(((done, back), (done_stats, back_stats))):
             copy = remote(

time: 64.2 us -> 59.9 us (0.933)
  Pallas kernels: 58.7 us -> 54.5 us
    pallas_call x1, Pallas kernels: 58.7 us -> 54.5 us  [per_device(): pl.pallas_call(functools.partial(body, count), out_shape=(jax.ShapeDtypeS...]
where the time goes in v5:
time: 59.9 us; the launch traced here: 59.7 us
  Pallas kernels  54.5 us (91%)
  local copies, waits for them, and re-layouts  3.33 us (6%)
  between operations  1.94 us (3%)
    pallas_call x1, Pallas kernels, per_device(): pl.pallas_call(functools.partial(body, count), out_shape=(jax.ShapeDtypeS...  54.5 us
    unnamed x4, local copies, waits for them, and re-layouts  3.33 us

profile of v5, /device:TPU:0, one launch (start us, length us, event | category | flops | bytes accessed | tf_op | source)
XLA Modules:
  0.0 59.7 jit_solution(6704186789874233503)
XLA Ops:
  1.9 54.5 %shard_map.104 = (bf16[256,1536]{1,0:T(8,128)(2,1)}, bf16[256,3072]{1,0:T(8,128)(2,1)}) custom-call(s32[1]{0:T(128)S(6)} %copy.13.timestep, s32[1]{0:T(128)S(6)} %copy.14.action, bf16[256,1536]{1,0:T(8,128)(2,1)} %latent.1, f32[9,1536]{1,0:T(8,128)} %conv_weight.1, bf16[50,4608]{1,0:T(8,128)(2,1)} %time_table.1, bf16[18,4608]{1,0:T(8,128)(2,1)} %action_table.1, ...), custom_call_target="tpu_custom_call" | custom-call | flops 8000000000 | bytes 31457280 | tf_op jit(solution)/shard_map/pallas_call | solution.py:765
  56.4 0.0 copy-start
  56.4 2.2 %copy.15 = bf16[256,1536]{1,0:T(8,128)(2,1)} copy(bf16[256,1536]{1,0:T(8,128)(2,1)} %get-tuple-element.4) | data formatting | bytes 1572864
  58.6 0.0 copy-done
  58.6 1.1 %copy.16 = bf16[256,3072]{1,0:T(8,128)(2,1)} copy(bf16[256,3072]{1,0:T(8,128)(2,1)S(1)} %copy-done) | data formatting | bytes 3145728
Async XLA Ops:
  56.4 2.2 %copy-start = (bf16[256,3072]{1,0:T(8,128)(2,1)S(1)}, bf16[256,3072]{1,0:T(8,128)(2,1)}, u32[]{:S(2)}) copy-start(bf16[256,3072]{1,0:T(8,128)(2,1)} %get-tuple-element.5) | copy-start | bytes 4718596

commit v6 on v5

--- a/solution.py
+++ b/solution.py
@@ -362,18 +362,20 @@
     return top, total, summed
 
 
-def pipeline(tasks, size, rows):
+def pipeline(tasks, size, rows, finish):
     states = {}
+    last = {task[0]: n for n, task in enumerate(tasks)}
     waiting = None
-    for task in tasks + [None]:
+    for n, task in enumerate(tasks + [None]):
         ahead = None
         if task is not None:
             ahead = jnp.dot(task[1](), task[3], preferred_element_type=jnp.float32)
         if waiting is not None:
             (stream, _, values, _), scores = waiting
             states[stream] = fold(states.get(stream), scores, values(), size, rows)
+            if last[stream] == n - 1:
+                finish(stream, states[stream])
         waiting = (task, ahead)
-    return states
 
 
 def blocked(flat, size, rows):
@@ -562,10 +564,11 @@
                 blocked(flat[i], size, rows),
             )
 
-        found = pipeline([task(u) for u in range(MANY)], size, rows)
-        for u in range(MANY):
+        def finish(u, state):
             i = g * MANY + u
-            tops[i], totals[i], acc[i] = found[u]
+            tops[i], totals[i], acc[i] = state
+
+        pipeline([task(u) for u in range(MANY)], size, rows, finish)
         return carry
 
     early = pairs // MANY - 1
@@ -629,37 +632,40 @@
                 [turned[i, :, pl.ds(slot * rows, rows)] for slot in chunk], axis=1
             )
 
-        tasks = [
-            (i, keys(chunk, i), values(chunk, i), queries[i])
-            for chunk in chunks
-            for i in range(mine)
-        ]
-        for i, (top, total, summed) in pipeline(tasks, size, rows).items():
-            result = (summed / total).astype(jnp.bfloat16)
+        order = [(i, chunk) for chunk in chunks for i in range(mine)]
+        if j == 1:
+            order = [(i, chunk) for i in range(mine) for chunk in chunks]
+        tasks = [(i, keys(chunk, i), values(chunk, i), queries[i]) for i, chunk in order]
+
+        def leave(src, dst, n):
+            copy = remote(
+                src, dst, back_send.at[j - 1, n], back_recv.at[j - 1, n], source(j) * 2 + core
+            )
+            copy.start()
+            sent.append(copy)
+            returning.setdefault(j, []).append(copy)
+
+        def finish(i, state):
+            top, total, summed = state
             place, stats = (back.at[0], back_stats.at[0])
             if j > 0:
                 place, stats = (done.at[j - 1], done_stats.at[j - 1])
-            place[i] = result
+            place[i] = (summed / total).astype(jnp.bfloat16)
             stats[i : i + 1, :] = top
             stats[mine + i : mine + i + 1, :] = total
-
+            if j > 0:
+                leave(done.at[j - 1, i], back.at[j, i], i)
+
+        pipeline(tasks, size, rows, finish)
+        if j > 0:
+            leave(done_stats.at[j - 1], back_stats.at[j], mine)
+
+    returning = {}
     serve(0)
     ready([0])
-    returning = []
     for j in range(chips - 1, 0, -1):
         asking[j].wait_recv()
         serve(j)
-        for n, (src, dst) in enumerate(((done, back), (done_stats, back_stats))):
-            copy = remote(
-                src.at[j - 1],
-                dst.at[j],
-                back_send.at[j - 1, n],
-                back_recv.at[j - 1, n],
-                source(j) * 2 + core,
-            )
-            copy.start()
-            sent.append(copy)
-            returning.append(copy)
 
     lax.fori_loop(early, pairs // MANY, local, 0)
 
@@ -681,7 +687,7 @@
 
     merge(0)
     for j in range(chips - 1, 0, -1):
-        for copy in returning[2 * (chips - 1 - j) : 2 * (chips - j)]:
+        for copy in returning[j]:
             copy.wait_recv()
         merge(j)
     loads[1].wait()
@@ -746,8 +752,8 @@
             dma((chips - 1,)),
             dma((chips - 1,)),
             dma((chips - 1,)),
-            dma((chips - 1, 2)),
-            dma((chips - 1, 2)),
+            dma((chips - 1, mine + 1)),
+            dma((chips - 1, mine + 1)),
             dma((4,)),
         ]
     else:

time: 59.9 us -> 58.5 us (0.977)
  Pallas kernels: 54.5 us -> 53 us
    pallas_call x1, Pallas kernels: 54.5 us -> 53 us  [per_device(): pl.pallas_call(functools.partial(body, count), out_shape=(jax.ShapeDtypeS...]
where the time goes in v6:
time: 58.5 us; the launch traced here: 58.3 us
  Pallas kernels  53 us (91%)
  local copies, waits for them, and re-layouts  3.33 us (6%)
  between operations  1.94 us (3%)
    pallas_call x1, Pallas kernels, per_device(): pl.pallas_call(functools.partial(body, count), out_shape=(jax.ShapeDtypeS...  53 us
    unnamed x4, local copies, waits for them, and re-layouts  3.33 us

profile of v6, /device:TPU:0, one launch (start us, length us, event | category | flops | bytes accessed | tf_op | source)
XLA Modules:
  0.0 58.3 jit_solution(6674822737077728784)
XLA Ops:
  1.9 53.0 %shard_map.104 = (bf16[256,1536]{1,0:T(8,128)(2,1)}, bf16[256,3072]{1,0:T(8,128)(2,1)}) custom-call(s32[1]{0:T(128)S(6)} %copy.13.timestep, s32[1]{0:T(128)S(6)} %copy.14.action, bf16[256,1536]{1,0:T(8,128)(2,1)} %latent.1, f32[9,1536]{1,0:T(8,128)} %conv_weight.1, bf16[50,4608]{1,0:T(8,128)(2,1)} %time_table.1, bf16[18,4608]{1,0:T(8,128)(2,1)} %action_table.1, ...), custom_call_target="tpu_custom_call" | custom-call | flops 8000000000 | bytes 31457280 | tf_op jit(solution)/shard_map/pallas_call | solution.py:771
  55.0 0.0 copy-start
  55.0 2.2 %copy.15 = bf16[256,1536]{1,0:T(8,128)(2,1)} copy(bf16[256,1536]{1,0:T(8,128)(2,1)} %get-tuple-element.4) | data formatting | bytes 1572864
  57.1 0.0 copy-done
  57.1 1.1 %copy.16 = bf16[256,3072]{1,0:T(8,128)(2,1)} copy(bf16[256,3072]{1,0:T(8,128)(2,1)S(1)} %copy-done) | data formatting | bytes 3145728
Async XLA Ops:
  55.0 2.2 %copy-start = (bf16[256,3072]{1,0:T(8,128)(2,1)S(1)}, bf16[256,3072]{1,0:T(8,128)(2,1)}, u32[]{:S(2)}) copy-start(bf16[256,3072]{1,0:T(8,128)(2,1)} %get-tuple-element.5) | copy-start | bytes 4718596
